TPU v7x, 256 devices: a whole 4x4x8 slice. The times are simulated.
256 devices in a mesh: bucket: 16 (over z, core), replica: 16 (over y, x).
Axes of the slice: x: 4, y: 4, z: 8, core: 2. Of those that a mesh axis runs over, the one named last changes fastest.
Arguments:
- rows: bfloat16 [262144, 768], P(('bucket', 'replica')), may hold values from -40 to 40, as said below
- cell_ids: int32 [262144, 1], P(('bucket', 'replica')), may hold values from 0 to 15; in each aligned block of 1024 rows (0 to 1023, 1024 to 2047, ...) at most 128 rows name the same one
- start_basis: float32 [16, 768, 768], P('bucket'), may hold values from -0.1 to 1.1, as said below
Outputs:
- rotated: bfloat16 [262144, 768], P(('bucket', 'replica'))
Inputs may be any that keep to these rules, and one draw needn't show every extreme that they name: `cell_ids`: in the rows of one device no cell is named by more than 128 rows, a bound that some block reaches; every cell is named by some row. `rows`: A residual row: a column offset plus rough noise with column and row scales. `start_basis`: the identity plus small dense entries.
All inputs are finite; a program needn't handle non-finite values.
Results may differ from a plain program's by a relative error of at most 0.0049.
Values may be sent and summed in bfloat16 or wider, within the bound.
A program may use at most 128 MiB of HBM per device.

v0:
```python
import jax
import jax.numpy as jnp
from jax import lax
from jax.sharding import PartitionSpec as P

CELLS = 16
ITERS_NS = 3
CAP = 128


def cell_solve(factor, image):
    return jax.scipy.linalg.solve_triangular(factor, image.T, lower=True).T


def local_gram(image):
    return jnp.einsum("cji,cjk->cik", image, image, precision=lax.Precision.HIGHEST)


def orthonormal(image, gram_matrix):
    factor = jax.vmap(jnp.linalg.cholesky)(gram_matrix)
    return jax.vmap(cell_solve)(factor, image)


def body(rows, cell_ids, start_basis):
    width = rows.shape[1]
    flat_ids = cell_ids[:, 0]
    onehot = (flat_ids[:, None] == jnp.arange(CELLS, dtype=jnp.int32)[None, :]).astype(jnp.int32)
    slot = jnp.sum(jnp.cumsum(onehot, axis=0) * onehot, axis=1) - 1
    send_counts = jnp.sum(onehot, axis=0).astype(jnp.bfloat16)[:, None]
    buffer = jnp.zeros((CELLS, CAP, width), jnp.bfloat16).at[flat_ids, slot].set(rows)
    received, recv_counts = (
        lax.all_to_all(buffer, "bucket", split_axis=0, concat_axis=1, tiled=True),
        lax.all_to_all(send_counts, "bucket", split_axis=0, concat_axis=1, tiled=True),
    )
    count_part = jnp.sum(recv_counts.astype(jnp.float32), axis=1)
    sum_part = jnp.sum(received, axis=1, dtype=jnp.float32)
    square_part = jnp.einsum("crd,cre->cde", received, received, preferred_element_type=jnp.float32)
    count_all, sum_all, square_all = lax.psum((count_part, sum_part, square_part), "replica")
    divisor = jnp.maximum(count_all, 1.0)
    mean = sum_all / divisor[:, None]
    covariance = square_all / divisor[:, None, None] - mean[:, :, None] * mean[:, None, :]
    current = start_basis
    for step in range(ITERS_NS):
        image = jnp.einsum("cij,cjk->cik", covariance, current, precision=lax.Precision.HIGHEST)
        current = orthonormal(image, local_gram(image))
    rotation = current.astype(jnp.bfloat16)
    shift = jnp.einsum(
        "cd,cde->ce", mean, rotation.astype(jnp.float32), precision=lax.Precision.HIGHEST
    )
    product = jnp.einsum("crd,cde->cre", received, rotation, preferred_element_type=jnp.float32)
    rotated_slots = (product - shift[:, None, :]).astype(jnp.bfloat16)
    returned = lax.all_to_all(rotated_slots, "bucket", split_axis=1, concat_axis=0, tiled=True)
    return returned[flat_ids, slot]


def solution(mesh):
    placed = (
        P(("bucket", "replica"), None),
        P(("bucket", "replica"), None),
        P("bucket", None, None),
    )
    return jax.shard_map(
        body, mesh=mesh, in_specs=placed, out_specs=P(("bucket", "replica"), None), check_vma=False
    )
```

profile of v0, /device:TPU:1, one launch (start us, length us, event | category | flops | bytes accessed | tf_op | source)
XLA Modules:
  0.0 1191.3 jit_solution(7130248097209281491)
XLA Ops:
  23.2 83.5 %all_to_all.31 = bf16[16,128,768]{2,1,0:T(8,128)(2,1)S(1)} all-to-all(bf16[16,128,768]{2,1,0:T(8,128)(2,1)} %bitcast.878), channel_id=1, replica_groups=mesh['bucket'=16,'replica'=16] {'bucket'}, dimensions={0} | all-to-all | bytes 6291456 | tf_op jit(solution)/shard_map/all_to_all | solution.py:32
  126.2 34.4 %all-reduce.1 = (f32[1,768]{1,0:T(1,128)S(1)}, f32[1]{0:T(128)}) all-reduce(f32[1,768]{1,0:T(1,128)S(1)} %reduce_sum.45, f32[1]{0:T(128)} %bitcast.11), channel_id=1, replica_groups=mesh['bucket'=16,'replica'=16] {'replica'}, use_global_device_ids=true, to_apply=%region_9.10 | all-reduce | flops 769 | bytes 6152 | tf_op jit(solution)/shard_map/psum | solution.py:38
  161.3 49.2 %all-reduce.4.cloned.1.call-done = f32[1,768,768]{2,1,0:T(8,128)} async-done(((f32[1,768,768]{2,1,0:T(8,128)}), f32[1,768,768]{2,1,0:T(8,128)}) %all-reduce.4.cloned.1.call-update) | async-done | bytes 2359312 | tf_op jit(solution)/shard_map/psum | solution.py:38
  254.9 11.7 custom-call.69
  278.6 11.7 custom-call.71
  302.7 12.1 %custom-call.73 = f32[1,128,128]{2,1,0:T(8,128)S(1)} custom-call(f32[1,128,128]{2,1,0:T(8,128)S(1)} %cholesky.930), custom_call_target="Cholesky" | custom-call | tf_op jit(solution)/shard_map/vmap(jit(cholesky))/cholesky | solution.py:20
  327.1 11.7 custom-call.75
  350.9 11.9 custom-call.77
  371.7 17.6 %while.6 = (s32[]{:T(128)}, f32[1,768,768]{2,1,0:T(8,128)}, s32[6,2]{0,1:T(2,128)S(1)}, f32[6,1,128,128]{3,2,1,0:T(8,128)S(1)}, s32[]{:T(128)}) while((s32[]{:T(128)}, f32[1,768,768]{2,1,0:T(8,128)}, s32[6,2]{0,1:T(2,128)S(1)}, f32[6,1,128,128]{3,2,1,0:T(8,128)S(1)}, s32[]{:T(128)}) %tuple.115), condition=%wide.while_cond, body=%wide.while_body.sunk | while | flops 2 | bytes 131181 | solution.py:12
  389.3 59.0 %custom-call.78 = f32[1,6,128,128]{2,3,1,0:T(8,128)S(1)} custom-call(f32[1,6,128,128]{3,2,1,0:T(8,128)S(1)} %bitcast.892), custom_call_target="InvertDiagBlocksLowerTriangular" | custom-call | tf_op jit(solution)/shard_map/vmap(jit(_solve_triangular))/triangular_solve | solution.py:12
  509.6 11.7 custom-call.81
  534.8 11.7 custom-call.83
  559.0 11.9 custom-call.85
  606.9 12.1 %custom-call.89 = f32[1,128,128]{2,1,0:T(8,128)S(1)} custom-call(f32[1,128,128]{2,1,0:T(8,128)S(1)} %fusion.139), custom_call_target="Cholesky" | custom-call | tf_op jit(solution)/shard_map/vmap(jit(cholesky))/cholesky | solution.py:20
  627.3 18.0 %while.7 = (s32[]{:T(128)}, f32[1,768,768]{2,1,0:T(8,128)}, s32[6,2]{0,1:T(2,128)S(1)}, f32[6,1,128,128]{3,2,1,0:T(8,128)S(1)}, s32[]{:T(128)}) while((s32[]{:T(128)}, f32[1,768,768]{2,1,0:T(8,128)}, s32[6,2]{0,1:T(2,128)S(1)}, f32[6,1,128,128]{3,2,1,0:T(8,128)S(1)}, s32[]{:T(128)}) %tuple.126), condition=%wide.while_cond.clone, body=%wide.while_body.clone.sunk | while | flops 2 | bytes 131181 | solution.py:12
  645.2 59.0 %custom-call.90 = f32[1,6,128,128]{2,3,1,0:T(8,128)S(1)} custom-call(f32[1,6,128,128]{3,2,1,0:T(8,128)S(1)} %bitcast.893), custom_call_target="InvertDiagBlocksLowerTriangular" | custom-call | tf_op jit(solution)/shard_map/vmap(jit(_solve_triangular))/triangular_solve | solution.py:12
  814.5 12.1 %custom-call.97 = f32[1,128,128]{2,1,0:T(8,128)S(1)} custom-call(f32[1,128,128]{2,1,0:T(8,128)S(1)} %cholesky.976), custom_call_target="Cholesky" | custom-call | tf_op jit(solution)/shard_map/vmap(jit(cholesky))/cholesky | solution.py:20
  862.7 11.9 custom-call.101
  882.7 16.8 %while.8 = (s32[]{:T(128)}, f32[1,768,768]{2,1,0:T(8,128)}, s32[6,2]{0,1:T(2,128)S(1)}, f32[6,1,128,128]{3,2,1,0:T(8,128)S(1)}, s32[]{:T(128)}) while((s32[]{:T(128)}, f32[1,768,768]{2,1,0:T(8,128)}, s32[6,2]{0,1:T(2,128)S(1)}, f32[6,1,128,128]{3,2,1,0:T(8,128)S(1)}, s32[]{:T(128)}) %tuple.127), condition=%wide.while_cond.clone.1, body=%wide.while_body.clone.1.sunk | while | flops 2 | bytes 131181 | solution.py:12
  899.5 59.0 %custom-call.102 = f32[1,6,128,128]{2,3,1,0:T(8,128)S(1)} custom-call(f32[1,6,128,128]{3,2,1,0:T(8,128)S(1)} %bitcast.891), custom_call_target="InvertDiagBlocksLowerTriangular" | custom-call | tf_op jit(solution)/shard_map/vmap(jit(_solve_triangular))/triangular_solve | solution.py:12
  980.9 44.7 %copy.127 = bf16[1,2048,768]{2,0,1:T(2,128)(2,1)} copy(bf16[1,2048,768]{2,1,0:T(8,128)(2,1)S(1)} %fusion) | data formatting | bytes 6291456 | tf_op jit(solution)/shard_map/convert_element_type | solution.py:51
  1026.2 33.3 %reduce.53 = bf16[2048,768]{1,0:T(8,128)(2,1)} reduce(bf16[2048,1,768]{2,1,0:T(2,128)(2,1)} %bitcast.875, bf16[]{:T(256)} %broadcast.362), dimensions={1}, to_apply=%bitcast.833.reduce_sub_computation | reduce | bytes 6291458
  1065.8 82.1 %all_to_all.32 = bf16[16,2,49152]{2,1,0:T(2,128)(2,1)} all-to-all(bf16[16,2,49152]{2,1,0:T(2,128)(2,1)} %reshape.753), channel_id=1, replica_groups=mesh['bucket'=16,'replica'=16] {'bucket'}, dimensions={0} | all-to-all | bytes 6291456 | tf_op jit(solution)/shard_map/all_to_all | solution.py:52
  1164.4 19.7 %gather_fusion = bf16[1024,768]{1,0:T(8,128)(2,1)} fusion(bf16[16,128,768]{2,1,0:T(8,128)(2,1)} %bitcast.852, s32[1024]{0:T(1024)S(1)} %bitcast.853), kind=kCustom, calls=%fused_computation | custom fusion | bytes 3153920 | tf_op jit(solution)/shard_map/gather | solution.py:53
  (280 shorter events, 509.7 us)
Async XLA Ops:
  6.5 204.0 %copy-start = (f32[1,768,768]{2,1,0:T(8,128)S(1)}, f32[1,768,768]{2,1,0:T(8,128)}, u32[]{:S(2)}) copy-start(f32[1,768,768]{2,1,0:T(8,128)} %param.8) | copy-start | bytes 7077892
  6.5 204.0 %all-reduce.4.cloned.1.call-start = ((), (), s32[]{:S(2)}) async-start(), calls=%async_computation.3 | async-start | bytes 4718592 | tf_op jit(solution)/shard_map/psum | solution.py:38
  106.7 1.7 copy-start.11
  113.2 9.8 all-to-all-start.1
  218.3 6.3 copy-start.4
  228.9 1.5 copy-start.15
  362.8 5.4 copy-start.8
  368.2 80.1 %copy-start.5 = (f32[768,768]{1,0:T(8,128)S(1)}, f32[768,768]{1,0:T(8,128)}, u32[]{:S(2)}) copy-start(f32[768,768]{1,0:T(8,128)} %copy-done.4) | copy-start | bytes 7077892
  461.0 6.0 copy-start.16
  473.1 6.5 copy-start.6
  483.6 1.5 copy-start.13
  619.1 4.7 copy-start.9
  623.8 80.4 %copy-start.7 = (f32[768,768]{1,0:T(8,128)S(1)}, f32[768,768]{1,0:T(8,128)}, u32[]{:S(2)}) copy-start(f32[768,768]{1,0:T(8,128)} %copy-done.6) | copy-start | bytes 7077892
  716.9 5.7 copy-start.17
  728.8 6.8 copy-start.2
  739.5 1.4 copy-start.14
  874.6 4.6 copy-start.10
  879.2 79.3 %copy-start.3 = (f32[768,768]{1,0:T(8,128)S(1)}, f32[768,768]{1,0:T(8,128)}, u32[]{:S(2)}) copy-start(f32[768,768]{1,0:T(8,128)} %copy-done.2) | copy-start | bytes 7077892
  971.7 6.3 copy-start.12
  1164.4 19.7 %copy-start.1 = (f32[1,768,768]{2,1,0:T(8,128)S(1)}, f32[1,768,768]{2,1,0:T(8,128)}, u32[]{:S(2)}) copy-start(f32[1,768,768]{2,1,0:T(8,128)} %param.8) | copy-start | bytes 7077892
Sparse Core Ops, SparseCore 0:
  112.6 97.8 all-reduce.3
where the time goes:
time: 1200 us; the launch traced here: 1190 us
  other arithmetic  611 us (51%)
  blocking collectives  200 us (17%)
  local copies, waits for them, and re-layouts  162 us (14%)
  matrix products  132 us (11%)
  waiting for transfers between devices  55.7 us (5%)
  between operations  27 us (2%)
    another operation x68, other arithmetic, orthonormal(): factor = jax.vmap(jnp.linalg.cholesky)(gram_matrix)  373 us
    another operation x7, other arithmetic, cell_solve(): return jax.scipy.linalg.solve_triangular(factor, image.T, lower=True).T  187 us
    all_to_all x1, blocking collectives, body(): lax.all_to_all(buffer, 'bucket', split_axis=0, concat_axis=1, tiled=True)  83.5 us
    all_to_all x1, blocking collectives, body(): lax.all_to_all(rotated_slots, 'bucket', split_axis=1, concat_axis=0, tile...  82.1 us
    another operation x33, matrix products, cell_solve(): return jax.scipy.linalg.solve_triangular(factor, image.T, lower=True).T  55.3 us
    another operation x58, local copies, waits for them, and re-layouts, cell_solve(): return jax.scipy.linalg.solve_triangular(factor, image.T, lower=True).T  52.1 us
    psum x1, waiting for transfers between devices, body(): lax.psum((count_part, sum_part, square_part), 'replica')  49.2 us
    convert_element_type x1, local copies, waits for them, and re-layouts, body(): rotated_slots = (product - shift[:, None, :]).astype(jnp.bfloat16)  44.7 us
  transfers between devices with their start and end apart: 2, of which 2 were waited for; matrix products, arithmetic and copies ran while one was open for 0% of the time, Pallas kernels for 0%

commit v1 on v0

--- a/solution.py
+++ b/solution.py
@@ -6,6 +6,29 @@
 CELLS = 16
 ITERS_NS = 3
 CAP = 128
+
+
+def in_blocks(shard, dim, size):
+    shape = shard.shape
+    blocks = shard.reshape(*shape[:dim], size, shape[dim] // size, *shape[dim + 1 :])
+    return jnp.moveaxis(blocks, dim, 0)
+
+
+def joined_along(blocks, dim):
+    blocks = jnp.moveaxis(blocks, 0, dim)
+    shape = blocks.shape
+    return blocks.reshape(*shape[:dim], shape[dim] * shape[dim + 1], *shape[dim + 2 :])
+
+
+def sent_to_each(array, axis, split_dim, concat_dim):
+    devices, mine = (lax.axis_size(axis), lax.axis_index(axis))
+    tiles = in_blocks(array, split_dim, devices)
+    done = [tiles[mine]]
+    for step in range(1, devices):
+        sent = tiles[(mine + step) % devices]
+        done.append(lax.ppermute(sent, axis, [(i, (i + step) % devices) for i in range(devices)]))
+    tiles = jnp.stack(done)[(mine - jnp.arange(devices)) % devices]
+    return joined_along(tiles, concat_dim)
 
 
 def cell_solve(factor, image):
@@ -49,7 +72,7 @@
     )
     product = jnp.einsum("crd,cde->cre", received, rotation, preferred_element_type=jnp.float32)
     rotated_slots = (product - shift[:, None, :]).astype(jnp.bfloat16)
-    returned = lax.all_to_all(rotated_slots, "bucket", split_axis=1, concat_axis=0, tiled=True)
+    returned = sent_to_each(rotated_slots, "bucket", 1, 0)
     return returned[flat_ids, slot]
 
 

time: 1200 us -> 1120 us (0.933)
  blocking collectives: 200 us -> 118 us
  local copies, waits for them, and re-layouts: 162 us -> 109 us
  starting transfers between devices: 3.37 us -> 54.3 us
  waiting for transfers between devices: 55.7 us -> 92.7 us
  other arithmetic: 611 us -> 577 us
    all_to_all x1 -> x0, blocking collectives: 82.1 us -> none  [body(): lax.all_to_all(rotated_slots, 'bucket', split_axis=1, concat_axis=0, tile...]
    ppermute x0 -> x15, starting transfers between devices: none -> 51 us  [sent_to_each(): lax.ppermute(sent, axis, [(i, (i + step) % devices) for i in range(device...]
    convert_element_type x1 -> x0, local copies, waits for them, and re-layouts: 44.7 us -> none  [body(): rotated_slots = (product - shift[:, None, :]).astype(jnp.bfloat16)]
    ppermute x0 -> x15, waiting for transfers between devices: none -> 37.2 us  [sent_to_each(): lax.ppermute(sent, axis, [(i, (i + step) % devices) for i in range(device...]
    unnamed x4 -> x3, other arithmetic: 34.8 us -> 1.5 us
    unnamed x41 -> x51, local copies, waits for them, and re-layouts: 37.3 us -> 23.5 us
  transfers between devices with their start and end apart: 2 -> 17, of which waited for: 2 -> 11; matrix products, arithmetic and copies ran while one was open for 0% -> 1% of each run, Pallas kernels for 0% -> 0%
where the time goes in v1:
time: 1120 us; the launch traced here: 1110 us
  other arithmetic  577 us (52%)
  matrix products  132 us (12%)
  blocking collectives  118 us (11%)
  local copies, waits for them, and re-layouts  109 us (10%)
  waiting for transfers between devices  92.7 us (8%)
  starting transfers between devices  54.3 us (5%)
  between operations  27.3 us (2%)
    another operation x68, other arithmetic, orthonormal(): factor = jax.vmap(jnp.linalg.cholesky)(gram_matrix)  373 us
    another operation x7, other arithmetic, cell_solve(): return jax.scipy.linalg.solve_triangular(factor, image.T, lower=True).T  187 us
    all_to_all x1, blocking collectives, body(): lax.all_to_all(buffer, 'bucket', split_axis=0, concat_axis=1, tiled=True)  83.5 us
    another operation x33, matrix products, cell_solve(): return jax.scipy.linalg.solve_triangular(factor, image.T, lower=True).T  55.3 us
    another operation x58, local copies, waits for them, and re-layouts, cell_solve(): return jax.scipy.linalg.solve_triangular(factor, image.T, lower=True).T  52.1 us
    ppermute x15, starting transfers between devices, sent_to_each(): lax.ppermute(sent, axis, [(i, (i + step) % devices) for i in range(device...  51 us
    psum x1, waiting for transfers between devices, body(): lax.psum((count_part, sum_part, square_part), 'replica')  49.2 us
    ppermute x15, waiting for transfers between devices, sent_to_each(): lax.ppermute(sent, axis, [(i, (i + step) % devices) for i in range(device...  37.2 us
  transfers between devices with their start and end apart: 17, of which 11 were waited for; matrix products, arithmetic and copies ran while one was open for 1% of the time, Pallas kernels for 0%

profile of v1, /device:TPU:1, one launch (start us, length us, event | category | flops | bytes accessed | tf_op | source)
XLA Modules:
  0.0 1111.9 jit_solution(12579782160741772296)
XLA Ops:
  23.2 83.5 %all_to_all.9 = bf16[16,128,768]{2,1,0:T(8,128)(2,1)S(1)} all-to-all(bf16[16,128,768]{2,1,0:T(8,128)(2,1)} %bitcast.932), channel_id=1, replica_groups=mesh['bucket'=16,'replica'=16] {'bucket'}, dimensions={0} | all-to-all | bytes 6291456 | tf_op jit(solution)/shard_map/all_to_all | solution.py:55
  126.2 34.4 %all-reduce.1 = (f32[1,768]{1,0:T(1,128)S(1)}, f32[1]{0:T(128)}) all-reduce(f32[1,768]{1,0:T(1,128)S(1)} %reduce_sum.45, f32[1]{0:T(128)} %bitcast.11), channel_id=1, replica_groups=mesh['bucket'=16,'replica'=16] {'replica'}, use_global_device_ids=true, to_apply=%region_9.10 | all-reduce | flops 769 | bytes 6152 | tf_op jit(solution)/shard_map/psum | solution.py:61
  161.3 49.2 %all-reduce.4.cloned.1.call-done = f32[1,768,768]{2,1,0:T(8,128)} async-done(((f32[1,768,768]{2,1,0:T(8,128)}), f32[1,768,768]{2,1,0:T(8,128)}) %all-reduce.4.cloned.1.call-update) | async-done | bytes 2359312 | tf_op jit(solution)/shard_map/psum | solution.py:61
  254.9 11.7 %custom-call.69 = f32[1,128,128]{2,1,0:T(8,128)S(1)} custom-call(f32[1,128,128]{2,1,0:T(8,128)S(1)} %cholesky.920), custom_call_target="Cholesky" | custom-call | tf_op jit(solution)/shard_map/vmap(jit(cholesky))/cholesky | solution.py:43
  278.6 11.7 %custom-call.71 = f32[1,128,128]{2,1,0:T(8,128)S(1)} custom-call(f32[1,128,128]{2,1,0:T(8,128)S(1)} %cholesky.925), custom_call_target="Cholesky" | custom-call | tf_op jit(solution)/shard_map/vmap(jit(cholesky))/cholesky | solution.py:43
  302.7 12.1 %custom-call.73 = f32[1,128,128]{2,1,0:T(8,128)S(1)} custom-call(f32[1,128,128]{2,1,0:T(8,128)S(1)} %cholesky.930), custom_call_target="Cholesky" | custom-call | tf_op jit(solution)/shard_map/vmap(jit(cholesky))/cholesky | solution.py:43
  327.1 11.7 %custom-call.75 = f32[1,128,128]{2,1,0:T(8,128)S(1)} custom-call(f32[1,128,128]{2,1,0:T(8,128)S(1)} %cholesky.935), custom_call_target="Cholesky" | custom-call | tf_op jit(solution)/shard_map/vmap(jit(cholesky))/cholesky | solution.py:43
  350.9 11.9 %custom-call.77 = f32[1,128,128]{2,1,0:T(8,128)S(1)} custom-call(f32[1,128,128]{2,1,0:T(8,128)S(1)} %fusion.137), custom_call_target="Cholesky" | custom-call | tf_op jit(solution)/shard_map/vmap(jit(cholesky))/cholesky | solution.py:43
  371.7 17.6 %while.6 = (s32[]{:T(128)}, f32[1,768,768]{2,1,0:T(8,128)}, s32[6,2]{0,1:T(2,128)S(1)}, f32[6,1,128,128]{3,2,1,0:T(8,128)S(1)}, s32[]{:T(128)}) while((s32[]{:T(128)}, f32[1,768,768]{2,1,0:T(8,128)}, s32[6,2]{0,1:T(2,128)S(1)}, f32[6,1,128,128]{3,2,1,0:T(8,128)S(1)}, s32[]{:T(128)}) %tuple.130), condition=%wide.while_cond, body=%wide.while_body.sunk | while | flops 2 | bytes 131181 | solution.py:35
  389.3 59.0 %custom-call.78 = f32[1,6,128,128]{2,3,1,0:T(8,128)S(1)} custom-call(f32[1,6,128,128]{3,2,1,0:T(8,128)S(1)} %bitcast.947), custom_call_target="InvertDiagBlocksLowerTriangular" | custom-call | tf_op jit(solution)/shard_map/vmap(jit(_solve_triangular))/triangular_solve | solution.py:35
  509.6 11.7 %custom-call.81 = f32[1,128,128]{2,1,0:T(8,128)S(1)} custom-call(f32[1,128,128]{2,1,0:T(8,128)S(1)} %cholesky.943), custom_call_target="Cholesky" | custom-call | tf_op jit(solution)/shard_map/vmap(jit(cholesky))/cholesky | solution.py:43
  534.8 11.7 %custom-call.83 = f32[1,128,128]{2,1,0:T(8,128)S(1)} custom-call(f32[1,128,128]{2,1,0:T(8,128)S(1)} %cholesky.948), custom_call_target="Cholesky" | custom-call | tf_op jit(solution)/shard_map/vmap(jit(cholesky))/cholesky | solution.py:43
  559.0 11.9 %custom-call.85 = f32[1,128,128]{2,1,0:T(8,128)S(1)} custom-call(f32[1,128,128]{2,1,0:T(8,128)S(1)} %cholesky.953), custom_call_target="Cholesky" | custom-call | tf_op jit(solution)/shard_map/vmap(jit(cholesky))/cholesky | solution.py:43
  583.1 11.7 %custom-call.87 = f32[1,128,128]{2,1,0:T(8,128)S(1)} custom-call(f32[1,128,128]{2,1,0:T(8,128)S(1)} %cholesky.958), custom_call_target="Cholesky" | custom-call | tf_op jit(solution)/shard_map/vmap(jit(cholesky))/cholesky | solution.py:43
  606.9 12.1 %custom-call.89 = f32[1,128,128]{2,1,0:T(8,128)S(1)} custom-call(f32[1,128,128]{2,1,0:T(8,128)S(1)} %fusion.138), custom_call_target="Cholesky" | custom-call | tf_op jit(solution)/shard_map/vmap(jit(cholesky))/cholesky | solution.py:43
  627.3 18.0 %while.7 = (s32[]{:T(128)}, f32[1,768,768]{2,1,0:T(8,128)}, s32[6,2]{0,1:T(2,128)S(1)}, f32[6,1,128,128]{3,2,1,0:T(8,128)S(1)}, s32[]{:T(128)}) while((s32[]{:T(128)}, f32[1,768,768]{2,1,0:T(8,128)}, s32[6,2]{0,1:T(2,128)S(1)}, f32[6,1,128,128]{3,2,1,0:T(8,128)S(1)}, s32[]{:T(128)}) %tuple.141), condition=%wide.while_cond.clone, body=%wide.while_body.clone.sunk | while | flops 2 | bytes 131181 | solution.py:35
  645.2 59.0 %custom-call.90 = f32[1,6,128,128]{2,3,1,0:T(8,128)S(1)} custom-call(f32[1,6,128,128]{3,2,1,0:T(8,128)S(1)} %bitcast.948), custom_call_target="InvertDiagBlocksLowerTriangular" | custom-call | tf_op jit(solution)/shard_map/vmap(jit(_solve_triangular))/triangular_solve | solution.py:35
  765.4 11.7 %custom-call.93 = f32[1,128,128]{2,1,0:T(8,128)S(1)} custom-call(f32[1,128,128]{2,1,0:T(8,128)S(1)} %cholesky.966), custom_call_target="Cholesky" | custom-call | tf_op jit(solution)/shard_map/vmap(jit(cholesky))/cholesky | solution.py:43
  814.5 12.1 %custom-call.97 = f32[1,128,128]{2,1,0:T(8,128)S(1)} custom-call(f32[1,128,128]{2,1,0:T(8,128)S(1)} %cholesky.976), custom_call_target="Cholesky" | custom-call | tf_op jit(solution)/shard_map/vmap(jit(cholesky))/cholesky | solution.py:43
  862.7 11.9 %custom-call.101 = f32[1,128,128]{2,1,0:T(8,128)S(1)} custom-call(f32[1,128,128]{2,1,0:T(8,128)S(1)} %fusion.139), custom_call_target="Cholesky" | custom-call | tf_op jit(solution)/shard_map/vmap(jit(cholesky))/cholesky | solution.py:43
  882.7 16.8 %while.8 = (s32[]{:T(128)}, f32[1,768,768]{2,1,0:T(8,128)}, s32[6,2]{0,1:T(2,128)S(1)}, f32[6,1,128,128]{3,2,1,0:T(8,128)S(1)}, s32[]{:T(128)}) while((s32[]{:T(128)}, f32[1,768,768]{2,1,0:T(8,128)}, s32[6,2]{0,1:T(2,128)S(1)}, f32[6,1,128,128]{3,2,1,0:T(8,128)S(1)}, s32[]{:T(128)}) %tuple.142), condition=%wide.while_cond.clone.1, body=%wide.while_body.clone.1.sunk | while | flops 2 | bytes 131181 | solution.py:35
  899.5 59.0 %custom-call.102 = f32[1,6,128,128]{2,3,1,0:T(8,128)S(1)} custom-call(f32[1,6,128,128]{3,2,1,0:T(8,128)S(1)} %bitcast.946), custom_call_target="InvertDiagBlocksLowerTriangular" | custom-call | tf_op jit(solution)/shard_map/vmap(jit(_solve_triangular))/triangular_solve | solution.py:35
  1039.6 20.3 %collective-permute-start.11 = (bf16[1,128,768]{2,1,0:T(8,128)(2,1)S(1)}, bf16[1,128,768]{2,1,0:T(8,128)(2,1)S(1)}, u32[]{:S(2)}, u32[]{:S(2)}) collective-permute-start(bf16[1,128,768]{2,1,0:T(8,128)(2,1)S(1)} %get-tuple-element.69), channel_id=1, source_target_pairs={{0,192},{16,208},{32,224},{48,240},{64,0},{80,16},{96,32},{112,48}... | collective-permute-start | bytes 589832 | tf_op jit(solution)/shard_map/ppermute | solution.py:29
  1084.9 19.8 %gather_fusion.1 = bf16[1024,768]{1,0:T(8,128)(2,1)} fusion(bf16[16,128,768]{2,1,0:T(8,128)(2,1)} %gather_fusion, s32[1024]{0:T(1024)S(1)} %bitcast.909), kind=kCustom, calls=%fused_computation.1 | custom fusion | bytes 3153920 | tf_op jit(solution)/shard_map/gather | solution.py:76
  (322 shorter events, 546.3 us)
Async XLA Ops:
  6.5 204.0 %copy-start = (f32[1,768,768]{2,1,0:T(8,128)S(1)}, f32[1,768,768]{2,1,0:T(8,128)}, u32[]{:S(2)}) copy-start(f32[1,768,768]{2,1,0:T(8,128)} %param.8) | copy-start | bytes 7077892
  6.5 204.0 %all-reduce.4.cloned.1.call-start = ((), (), s32[]{:S(2)}) async-start(), calls=%async_computation.2 | async-start | bytes 4718592 | tf_op jit(solution)/shard_map/psum | solution.py:61
  113.2 9.8 all-to-all-start.1
  368.2 80.1 %copy-start.5 = (f32[768,768]{1,0:T(8,128)S(1)}, f32[768,768]{1,0:T(8,128)}, u32[]{:S(2)}) copy-start(f32[768,768]{1,0:T(8,128)} %copy-done.4) | copy-start | bytes 7077892
  473.1 6.5 copy-start.6
  623.8 80.4 %copy-start.7 = (f32[768,768]{1,0:T(8,128)S(1)}, f32[768,768]{1,0:T(8,128)}, u32[]{:S(2)}) copy-start(f32[768,768]{1,0:T(8,128)} %copy-done.6) | copy-start | bytes 7077892
  728.8 6.8 copy-start.2
  879.2 79.3 %copy-start.3 = (f32[768,768]{1,0:T(8,128)S(1)}, f32[768,768]{1,0:T(8,128)}, u32[]{:S(2)}) copy-start(f32[768,768]{1,0:T(8,128)} %copy-done.2) | copy-start | bytes 7077892
  982.0 8.7 collective-permute-start
  984.6 10.0 collective-permute-start.1
  986.0 13.6 %collective-permute-start.2 = (bf16[1,128,768]{2,1,0:T(8,128)(2,1)S(1)}, bf16[1,128,768]{2,1,0:T(8,128)(2,1)S(1)}, u32[]{:S(2)}, u32[]{:S(2)}) collective-permute-start(bf16[1,128,768]{2,1,0:T(8,128)(2,1)S(1)} %get-tuple-element.78), channel_id=1, source_target_pairs={{0,48},{16,64},{32,80},{48,96},{64,112},{80,128},{96,144},{112,160... | collective-permute-start | bytes 589832 | tf_op jit(solution)/shard_map/ppermute | solution.py:29
  987.3 19.6 %collective-permute-start.3 = (bf16[1,128,768]{2,1,0:T(8,128)(2,1)S(1)}, bf16[1,128,768]{2,1,0:T(8,128)(2,1)S(1)}, u32[]{:S(2)}, u32[]{:S(2)}) collective-permute-start(bf16[1,128,768]{2,1,0:T(8,128)(2,1)S(1)} %get-tuple-element.77), channel_id=1, source_target_pairs={{0,64},{16,80},{32,96},{48,112},{64,128},{80,144},{96,160},{112,17... | collective-permute-start | bytes 589832 | tf_op jit(solution)/shard_map/ppermute | solution.py:29
  989.8 29.5 %collective-permute-start.4 = (bf16[1,128,768]{2,1,0:T(8,128)(2,1)S(1)}, bf16[1,128,768]{2,1,0:T(8,128)(2,1)S(1)}, u32[]{:S(2)}, u32[]{:S(2)}) collective-permute-start(bf16[1,128,768]{2,1,0:T(8,128)(2,1)S(1)} %get-tuple-element.76), channel_id=1, source_target_pairs={{0,80},{16,96},{32,112},{48,128},{64,144},{80,160},{96,176},{112,1... | collective-permute-start | bytes 589832 | tf_op jit(solution)/shard_map/ppermute | solution.py:29
  990.7 44.4 %collective-permute-start.5 = (bf16[1,128,768]{2,1,0:T(8,128)(2,1)S(1)}, bf16[1,128,768]{2,1,0:T(8,128)(2,1)S(1)}, u32[]{:S(2)}, u32[]{:S(2)}) collective-permute-start(bf16[1,128,768]{2,1,0:T(8,128)(2,1)S(1)} %get-tuple-element.75), channel_id=1, source_target_pairs={{0,96},{16,112},{32,128},{48,144},{64,160},{80,176},{96,192},{112,... | collective-permute-start | bytes 589832 | tf_op jit(solution)/shard_map/ppermute | solution.py:29
  994.7 44.9 %collective-permute-start.6 = (bf16[1,128,768]{2,1,0:T(8,128)(2,1)S(1)}, bf16[1,128,768]{2,1,0:T(8,128)(2,1)S(1)}, u32[]{:S(2)}, u32[]{:S(2)}) collective-permute-start(bf16[1,128,768]{2,1,0:T(8,128)(2,1)S(1)} %get-tuple-element.74), channel_id=1, source_target_pairs={{0,112},{16,128},{32,144},{48,160},{64,176},{80,192},{96,208},{112... | collective-permute-start | bytes 589832 | tf_op jit(solution)/shard_map/ppermute | solution.py:29
  999.6 61.1 %collective-permute-start.7 = (bf16[1,128,768]{2,1,0:T(8,128)(2,1)S(1)}, bf16[1,128,768]{2,1,0:T(8,128)(2,1)S(1)}, u32[]{:S(2)}, u32[]{:S(2)}) collective-permute-start(bf16[1,128,768]{2,1,0:T(8,128)(2,1)S(1)} %get-tuple-element.73), channel_id=1, source_target_pairs={{0,128},{16,144},{32,160},{48,176},{64,192},{80,208},{96,224},{112... | collective-permute-start | bytes 589832 | tf_op jit(solution)/shard_map/ppermute | solution.py:29
  1006.9 54.4 %collective-permute-start.8 = (bf16[1,128,768]{2,1,0:T(8,128)(2,1)S(1)}, bf16[1,128,768]{2,1,0:T(8,128)(2,1)S(1)}, u32[]{:S(2)}, u32[]{:S(2)}) collective-permute-start(bf16[1,128,768]{2,1,0:T(8,128)(2,1)S(1)} %get-tuple-element.72), channel_id=1, source_target_pairs={{0,144},{16,160},{32,176},{48,192},{64,208},{80,224},{96,240},{112... | collective-permute-start | bytes 589832 | tf_op jit(solution)/shard_map/ppermute | solution.py:29
  1019.4 42.6 %collective-permute-start.9 = (bf16[1,128,768]{2,1,0:T(8,128)(2,1)S(1)}, bf16[1,128,768]{2,1,0:T(8,128)(2,1)S(1)}, u32[]{:S(2)}, u32[]{:S(2)}) collective-permute-start(bf16[1,128,768]{2,1,0:T(8,128)(2,1)S(1)} %get-tuple-element.71), channel_id=1, source_target_pairs={{0,160},{16,176},{32,192},{48,208},{64,224},{80,240},{96,0},{112,1... | collective-permute-start | bytes 589832 | tf_op jit(solution)/shard_map/ppermute | solution.py:29
  1035.1 28.0 %collective-permute-start.10 = (bf16[1,128,768]{2,1,0:T(8,128)(2,1)S(1)}, bf16[1,128,768]{2,1,0:T(8,128)(2,1)S(1)}, u32[]{:S(2)}, u32[]{:S(2)}) collective-permute-start(bf16[1,128,768]{2,1,0:T(8,128)(2,1)S(1)} %get-tuple-element.70), channel_id=1, source_target_pairs={{0,176},{16,192},{32,208},{48,224},{64,240},{80,0},{96,16},{112,32... | collective-permute-start | bytes 589832 | tf_op jit(solution)/shard_map/ppermute | solution.py:29
  1039.6 27.5 %collective-permute-start.11 = (bf16[1,128,768]{2,1,0:T(8,128)(2,1)S(1)}, bf16[1,128,768]{2,1,0:T(8,128)(2,1)S(1)}, u32[]{:S(2)}, u32[]{:S(2)}) collective-permute-start(bf16[1,128,768]{2,1,0:T(8,128)(2,1)S(1)} %get-tuple-element.69), channel_id=1, source_target_pairs={{0,192},{16,208},{32,224},{48,240},{64,0},{80,16},{96,32},{112,48}... | collective-permute-start | bytes 589832 | tf_op jit(solution)/shard_map/ppermute | solution.py:29
  1060.6 14.2 %collective-permute-start.12 = (bf16[1,128,768]{2,1,0:T(8,128)(2,1)S(1)}, bf16[1,128,768]{2,1,0:T(8,128)(2,1)S(1)}, u32[]{:S(2)}, u32[]{:S(2)}) collective-permute-start(bf16[1,128,768]{2,1,0:T(8,128)(2,1)S(1)} %get-tuple-element.68), channel_id=1, source_target_pairs={{0,208},{16,224},{32,240},{48,0},{64,16},{80,32},{96,48},{112,64},... | collective-permute-start | bytes 589832 | tf_op jit(solution)/shard_map/ppermute | solution.py:29
  1061.3 17.8 %collective-permute-start.13 = (bf16[1,128,768]{2,1,0:T(8,128)(2,1)S(1)}, bf16[1,128,768]{2,1,0:T(8,128)(2,1)S(1)}, u32[]{:S(2)}, u32[]{:S(2)}) collective-permute-start(bf16[1,128,768]{2,1,0:T(8,128)(2,1)S(1)} %get-tuple-element.67), channel_id=1, source_target_pairs={{0,224},{16,240},{32,0},{48,16},{64,32},{80,48},{96,64},{112,80},{... | collective-permute-start | bytes 589832 | tf_op jit(solution)/shard_map/ppermute | solution.py:29
  1062.0 17.8 %collective-permute-start.14 = (bf16[1,128,768]{2,1,0:T(8,128)(2,1)S(1)}, bf16[1,128,768]{2,1,0:T(8,128)(2,1)S(1)}, u32[]{:S(2)}, u32[]{:S(2)}) collective-permute-start(bf16[1,128,768]{2,1,0:T(8,128)(2,1)S(1)} %get-tuple-element.66), channel_id=1, source_target_pairs={{0,240},{16,0},{32,16},{48,32},{64,48},{80,64},{96,80},{112,96},{1... | collective-permute-start | bytes 589832 | tf_op jit(solution)/shard_map/ppermute | solution.py:29
  1084.9 19.8 %copy-start.1 = (f32[1,768,768]{2,1,0:T(8,128)S(1)}, f32[1,768,768]{2,1,0:T(8,128)}, u32[]{:S(2)}) copy-start(f32[1,768,768]{2,1,0:T(8,128)} %param.8) | copy-start | bytes 7077892
  (11 other events, 45.1 us)
Sparse Core Ops, SparseCore 0:
  112.6 97.8 all-reduce.3
